TPU v7x, 256 devices: a whole 4x4x8 slice. The times are simulated.
256 devices in a mesh: dp: 8 (over y_hi, x), tensor: 8 (over z), owner: 4 (over y_lo, core).
Axes of the slice: x: 4, y: 4 (y_hi: 2, y_lo: 2; y = y_hi * 2 + y_lo), z: 8, core: 2. Of those that a mesh axis runs over, the one named last changes fastest.
Arguments:
- acts: bfloat16 [8192, 6144], P('dp', 'owner'), may hold values from -80 to 80
- outgrads: bfloat16 [8192, 12288], P('dp', 'tensor'), may hold values from -80 to 80
- a_inverse: bfloat16 [4, 1536, 1536], P('owner', ('dp', 'tensor')), may hold values from -2.3784142 to 11.892071
- g_inverse: bfloat16 [8, 1536, 1536], P('tensor'), may hold values from -2.3784142 to 11.892071
Outputs:
- act_cov: float32 [4, 1536, 1536], P('owner', ('dp', 'tensor'))
- grad_cov: float32 [8, 1536, 1536], P('tensor', ('dp', 'owner'))
- precond: bfloat16 [4, 1536, 12288], P('owner', 'dp', 'tensor')
All inputs are finite; a program needn't handle non-finite values.
Results may differ from a plain program's by a relative error of at most 0.029.
Values may be sent and summed in bfloat16 or wider, within the bound.
A program may use at most 128 MiB of HBM per device.

v0:
```python
import jax
import jax.numpy as jnp
from jax import lax
from jax.sharding import PartitionSpec as P


def cross(left, right):
    return lax.dot_general(
        left, right, (((0,), (0,)), ((), ())), preferred_element_type=jnp.float32
    )


def per_device(acts, outgrads, a_inverse, g_inverse):
    n_data = lax.axis_size("dp")
    n_tensor = lax.axis_size("tensor")
    n_owner = lax.axis_size("owner")
    tok_rows = acts.shape[0]
    total = tok_rows * n_data
    tensor_index = lax.axis_index("tensor")
    owner_index = lax.axis_index("owner")
    a_share = tok_rows // n_tensor
    a_part = lax.dynamic_slice_in_dim(acts, tensor_index * a_share, a_share, 0)
    act_cov = lax.psum_scatter(
        cross(a_part, a_part) / total, ("dp", "tensor"), scatter_dimension=0, tiled=True
    )
    g_share = tok_rows // n_owner
    g_part = lax.dynamic_slice_in_dim(outgrads, owner_index * g_share, g_share, 0)
    grad_cov = lax.psum_scatter(
        (cross(g_part, g_part) / total).astype(jnp.bfloat16),
        ("dp", "owner"),
        scatter_dimension=0,
        tiled=True,
    ).astype(jnp.float32)
    columns = acts
    gradient = lax.psum_scatter(
        (cross(columns, outgrads) / total).astype(jnp.bfloat16),
        "dp",
        scatter_dimension=0,
        tiled=True,
    )
    right = jnp.dot(gradient, g_inverse[0], preferred_element_type=jnp.float32).astype(jnp.bfloat16)
    inverse_panel = lax.all_gather(a_inverse[0], "tensor", axis=0, tiled=True)
    columns = inverse_panel
    precond = jnp.dot(
        columns, lax.all_gather(right, "dp", axis=0, tiled=True), preferred_element_type=jnp.float32
    )
    return (act_cov[None], grad_cov[None], precond.astype(jnp.bfloat16)[None])


def solution(mesh):
    return jax.shard_map(
        per_device,
        mesh=mesh,
        in_specs=(
            P("dp", "owner"),
            P("dp", "tensor"),
            P("owner", ("dp", "tensor"), None),
            P("tensor", None, None),
        ),
        out_specs=(
            P("owner", ("dp", "tensor"), None),
            P("tensor", ("dp", "owner"), None),
            P("owner", "dp", "tensor"),
        ),
        check_vma=False,
    )
```

profile of v0, /device:TPU:2, one launch (start us, length us, event | category | flops | bytes accessed | tf_op | source)
XLA Modules:
  0.0 1164.5 jit_solution(6874784719201592880)
XLA Ops:
  7.2 0.0 copy-start
  7.2 0.0 reduce-scatter.8.cloned.1.call-start
  7.2 1.8 copy-done
  9.1 8.8 fusion
  17.8 0.0 reduce-scatter.8.cloned.1.call-update
  17.9 0.0 reduce-scatter.6.cloned.1.call-start
  17.9 3.7 fusion.1
  21.6 0.0 reduce-scatter.6.cloned.1.call-update
  21.6 0.0 all-gather.3.cloned.1.call-start
  21.7 92.4 %reduce-scatter.8.cloned.1.call-done = bf16[192,1536]{1,0:T(8,128)(2,1)} async-done(((bf16[1536,1536]{1,0:T(8,128)(2,1)}), bf16[192,1536]{1,0:T(8,128)(2,1)}) %reduce-scatter.8.cloned.1.call-update) | async-done | bytes 589840 | tf_op jit(solution)/shard_map/reduce_scatter | solution.py:35
  114.1 4.4 fusion.4
  118.5 0.0 all-gather.3.cloned.1.call-update
  118.5 0.0 reduce-scatter.4.cloned.1.call-start
  118.6 6.1 convolution_multiply_fusion.1
  124.7 0.0 copy-start.1
  124.7 0.0 reduce-scatter.4.cloned.1.call-update
  124.7 0.9 copy-done.1
  125.6 29.3 %all-gather = bf16[1,192,1536]{2,1,0:T(8,128)(2,1)} all-gather(bf16[1,24,1536]{2,1,0:T(8,128)(2,1)S(1)} %copy-done.1), channel_id=2, replica_groups=mesh['dp'=8,'tensor'=8,'owner'=4] {'tensor'}, dimensions={1}, use_global_device_ids=true | all-gather | bytes 663552 | tf_op jit(solution)/shard_map/all_gather | solution.py:42
  154.9 93.4 %reduce-scatter.6.cloned.1.call-done = bf16[48,1536]{1,0:T(8,128)(2,1)} async-done(((bf16[1536,1536]{1,0:T(8,128)(2,1)}), bf16[48,1536]{1,0:T(8,128)(2,1)}) %reduce-scatter.6.cloned.1.call-update) | async-done | bytes 147472 | tf_op jit(solution)/shard_map/reduce_scatter | solution.py:28
  248.3 1.6 bitcast_convert_fusion
  250.0 87.3 %all-gather.3.cloned.1.call-done = bf16[1536,1536]{1,0:T(8,128)(2,1)} async-done(((bf16[192,1536]{1,0:T(8,128)(2,1)}), bf16[1536,1536]{1,0:T(8,128)(2,1)}) %all-gather.3.cloned.1.call-update) | async-done | bytes 4718608 | tf_op jit(solution)/shard_map/all_gather | solution.py:45
  337.3 4.4 fusion.7
  341.7 816.2 %reduce-scatter.4.cloned.1.call-done = f32[24,1536]{1,0:T(8,128)} async-done(((f32[1536,1536]{1,0:T(8,128)}), f32[24,1536]{1,0:T(8,128)}) %reduce-scatter.4.cloned.1.call-update) | async-done | bytes 147472 | tf_op jit(solution)/shard_map/reduce_scatter | solution.py:23
Async XLA Ops:
  7.2 1.9 copy-start
  7.2 106.9 %reduce-scatter.8.cloned.1.call-start = ((), (), s32[]{:S(2)}) async-start(), calls=%async_computation.5 | async-start | bytes 5308416 | tf_op jit(solution)/shard_map/reduce_scatter | solution.py:35
  17.9 230.5 %reduce-scatter.6.cloned.1.call-start = ((), (), s32[]{:S(2)}) async-start(), calls=%async_computation.4 | async-start | bytes 4866048 | tf_op jit(solution)/shard_map/reduce_scatter | solution.py:28
  21.6 315.7 %all-gather.3.cloned.1.call-start = ((), (), s32[]{:S(2)}) async-start(), calls=%async_computation.6 | async-start | bytes 5308416 | tf_op jit(solution)/shard_map/all_gather | solution.py:45
  118.5 1039.4 %reduce-scatter.4.cloned.1.call-start = ((), (), s32[]{:S(2)}) async-start(), calls=%async_computation.3 | async-start | bytes 9584640 | tf_op jit(solution)/shard_map/reduce_scatter | solution.py:23
  124.7 0.9 copy-start.1
Sparse Core Ops, SparseCore 0:
  18.0 96.0 reduce-scatter.7
  116.8 131.5 reduce-scatter.5
  251.8 85.4 all-gather.2
  344.5 813.3 reduce-scatter.3
where the time goes:
time: 1160 us
  waiting for transfers between devices  1090 us (94%)
  blocking collectives  29.3 us (3%)
  matrix products  27.4 us (2%)
  between operations  13.8 us (1%)
    reduce_scatter x1, waiting for transfers between devices, per_device(): lax.psum_scatter(cross(a_part, a_part) / total, ('dp', 'tensor'), scatter...  816 us
    reduce_scatter x1, waiting for transfers between devices, per_device(): lax.psum_scatter((cross(g_part, g_part) / total).astype(jnp.bfloat16), ('...  93.4 us
    reduce_scatter x1, waiting for transfers between devices, per_device(): lax.psum_scatter((cross(columns, outgrads) / total).astype(jnp.bfloat16),...  92.4 us
    all_gather x1, waiting for transfers between devices, per_device(): lax.all_gather(right, 'dp', axis=0, tiled=True)  87.3 us
    all_gather x1, blocking collectives, per_device(): inverse_panel = lax.all_gather(a_inverse[0], 'tensor', axis=0, tiled=True)  29.3 us
  transfers between devices with their start and end apart: 4, of which 4 were waited for; matrix products, arithmetic and copies ran while one was open for 2% of the time, Pallas kernels for 0%

commit v1 on v0

v1 whole, which is shorter than its diff:
```python
import functools

import jax
import jax.numpy as jnp
from jax import lax
from jax.experimental import pallas as pl
from jax.experimental.pallas import tpu as pltpu
from jax.sharding import PartitionSpec as P

MESH = pl.DeviceIdType.MESH
BF = jnp.bfloat16
F32 = jnp.float32
BLK = 1536
TOK = 1024
SCALE = 1.0 / 8192.0
NX, NZ = 4, 8
CH = BLK // NX
HF = CH // 2
PC = 512
NP = BLK // PC
PEERS = ((1, 0), (3, 0), (0, 1), (2, 0), (1, 1), (3, 1), (2, 1))


def nt(a, b):
    return lax.dot_general(a, b, (((1,), (1,)), ((), ())), preferred_element_type=F32)


def nn(a, b):
    return jnp.dot(a, b, preferred_element_type=F32)


def kernel(
    acts_h, og_h, a_ref, b_h,
    act_out, grad_out, pre_out,
    acts, og, ogt, bv, a48, ra, abuf,
    u1, u2, u3, r1, r2, r3, keep, own, ys, yr, gt,
    pg, pa, rg, ra_c, sg, sa, xg, xa,
    hf, hb, rh, acc,
    lsem, ssem, rsem,
):
    d = lax.axis_index("dp")
    t = lax.axis_index("tensor")
    o = lax.axis_index("owner")
    x = lax.rem(d, NX)
    h = lax.div(d, NX)

    def dp_dev(dx, dh):
        return (lax.rem(h + dh, 2) * NX + lax.rem(x + dx, NX), t, o)

    def z_dev(dz):
        return (d, lax.rem(t + dz + NZ, NZ), o)

    def neg(off):
        return ((NX - off[0]) % NX, off[1])

    counter = [0]
    sends = []

    def send(src, dst, dev):
        i = counter[0]
        counter[0] += 1
        copy = pltpu.make_async_remote_copy(
            src_ref=src, dst_ref=dst, send_sem=ssem.at[i], recv_sem=rsem.at[i],
            device_id=dev, device_id_type=MESH,
        )
        copy.start()
        sends.append(copy)
        return copy

    rel = [lax.rem(x + k, NX) for k in (2, 1, 3, 0)]
    cols = [pl.ds(pl.multiple_of(r * CH, CH), CH) for r in rel]

    local = []

    def load(src, dst):
        copy = pltpu.make_async_copy(src, dst, lsem.at[len(local)])
        copy.start()
        local.append(copy)
        return copy

    load_og = [load(og_h.at[:, cols[0]], og.at[:, cols[0]])]
    load_acts = load(acts_h, acts)
    for k in range(1, 4):
        load_og.append(load(og_h.at[:, cols[k]], og.at[:, cols[k]]))
    load_b = load(b_h.at[0], bv)

    barrier = pltpu.get_barrier_semaphore()
    for off in PEERS:
        pl.semaphore_signal(barrier, inc=1, device_id=dp_dev(*off), device_id_type=MESH)
    for dz in (1, -1):
        pl.semaphore_signal(barrier, inc=1, device_id=z_dev(dz), device_id_type=MESH)
    a32 = a_ref[0].astype(F32)
    a48[...] = jnp.concatenate([a32[:, : BLK // 2], a32[:, BLK // 2 :]], axis=0).astype(BF)
    pl.semaphore_wait(barrier, len(PEERS) + 2)

    a_copies = [send(a48, ra.at[k], dp_dev(*off)) for k, off in enumerate(PEERS)]

    xp, xm = dp_dev(1, 0), dp_dev(3, 0)
    pieces = [pl.ds(p * PC, PC) for p in range(NP)]

    def turn(k):
        load_og[k].wait()
        ogt[cols[k], :] = og[:, cols[k]].T

    def product(k, p):
        return nn(ogt[cols[k], :], acts[:, pieces[p]]) * SCALE

    turn(0)
    load_acts.wait()
    c1 = []
    for p in range(NP):
        g = product(0, p).astype(BF)
        u1[0, :, pieces[p]] = g[:HF]
        u1[1, :, pieces[p]] = g[HF:]
        c1.append(
            [
                send(u1.at[0, :, pieces[p]], r1.at[0, :, pieces[p]], xp),
                send(u1.at[1, :, pieces[p]], r1.at[1, :, pieces[p]], xm),
            ]
        )
    c2 = [[None, None] for _ in range(NP)]
    for side in range(2):
        turn(1 + side)
        for p in range(NP):
            g = product(1 + side, p)
            now, later = (g[HF:], g[:HF]) if side == 0 else (g[:HF], g[HF:])
            u2[side, :, pieces[p]] = now.astype(BF)
            c2[p][side] = send(
                u2.at[side, :, pieces[p]], r2.at[side, :, pieces[p]], (xp, xm)[side]
            )
            keep[side, :, pieces[p]] = later

    half = BLK // 2
    rows = [a_ref[0].astype(F32)]
    for k in range(len(PEERS)):
        a_copies[k].wait_recv()
        v = ra[k].astype(F32)
        rows.append(jnp.concatenate([v[:24], v[24:]], axis=1))
    abuf[t] = jnp.concatenate(rows, axis=0).astype(BF)
    up, down = z_dev(1), z_dev(-1)

    def ring(slot, dev, part=None):
        ref = abuf.at[slot] if part is None else abuf.at[slot, part]
        return send(ref, ref, dev)

    def arrived(copy):
        copy.wait_recv()

    zc = [(ring(t, up), ring(t, down))]

    turn(3)
    gsel = jnp.concatenate(
        [ogt[pl.ds(pl.multiple_of(j * 192 + o * 48, 16), 48), :] for j in range(8)], axis=0
    )
    for p in range(NP):
        r = (nn(gsel, og[:, pieces[p]]) * SCALE).astype(BF)
        pg[:, :, pieces[p]] = r.reshape(8, 48, PC)
    yd = dp_dev(0, 1)
    there, here = (1 - h) * NX, h * NX
    cg = send(pg.at[pl.ds(there, NX)], rg, yd)
    j = lax.broadcasted_iota(jnp.int32, (256, BLK), 0)
    i = lax.broadcasted_iota(jnp.int32, (256, BLK), 1)
    r = lax.rem(j, 32)
    pick = (i == lax.div(j, 32) * 192 + t * 24 + r) & (r < 24)
    asel = nt(jnp.where(pick, 1.0, 0.0).astype(BF), acts[...]).astype(BF)
    for p in range(NP):
        v = (nn(asel, acts[:, pieces[p]]) * SCALE).astype(BF)
        pa[:, :, pieces[p]] = v.reshape(8, 32, PC)
    ca = send(pa.at[pl.ds(there, NX)], ra_c, yd)
    for p in range(NP):
        g = product(3, p)
        own[0, :, pieces[p]] = g[:HF]
        own[1, :, pieces[p]] = g[HF:]

    c3 = []
    for p in range(NP):
        row = []
        for side in range(2):
            c1[p][side].wait_recv()
            u3[side, :, pieces[p]] = (
                keep[side, :, pieces[p]] + r1[side, :, pieces[p]].astype(F32)
            ).astype(BF)
            row.append(
                send(u3.at[side, :, pieces[p]], r3.at[side, :, pieces[p]], (xp, xm)[side])
            )
        c3.append(row)

    def pass_on(s):
        a, b = zc[s - 1]
        lower, upper = lax.rem(t - s + NZ, NZ), lax.rem(t + s, NZ)
        a.wait_recv()
        first, second = (None, None) if s < 3 else (pl.ds(0, 96), pl.ds(96, 96))
        fa = ring(lower, up, first)
        b.wait_recv()
        fb = ring(upper, down, second)
        zc.append((fa, fb))

    pass_on(1)

    cg.wait_recv()
    ca.wait_recv()
    cx = []
    for k in range(1, NX):
        q = lax.rem(x + k, NX)
        sg[k - 1] = (pg[here + q].astype(F32) + rg[q].astype(F32)).astype(BF)
        sa[k - 1] = (pa[here + q].astype(F32) + ra_c[q].astype(F32)).astype(BF)
        cx.append(send(sg.at[k - 1], xg.at[k - 1], dp_dev(k, 0)))
        cx.append(send(sa.at[k - 1], xa.at[k - 1], dp_dev(k, 0)))

    cy = []
    for p in range(NP):
        for side in range(2):
            c2[p][side].wait_recv()
            c3[p][side].wait_recv()
        w = pieces[p]
        q = 1 - h
        ys[:, w] = (own[q, :, w] + r2[h, :, w].astype(F32) + r3[q, :, w].astype(F32)).astype(BF)
        cy.append(send(ys.at[:, w], yr.at[:, w], yd))
        own[h, :, w] = own[h, :, w] + r2[q, :, w].astype(F32) + r3[h, :, w].astype(F32)
    pass_on(2)
    for p in range(NP):
        w = pieces[p]
        cy[p].wait_recv()
        gt[:, w] = (own[h, :, w] + yr[:, w].astype(F32)).astype(BF)

    def left(slot):
        v = nt(abuf[slot], gt[...])
        at = pl.ds(pl.multiple_of(slot * 24, 8), 24)
        for k in range(8):
            hf[k, at, :] = v[k * 24 : (k + 1) * 24]

    for s in (0, -1, 1, -2, 2):
        left(lax.rem(t + s + NZ, NZ))
    pass_on(3)
    for s in (-3, 3):
        left(lax.rem(t + s + NZ, NZ))

    for c in cx:
        c.wait_recv()
    vg = pg[d].astype(F32) + rg[x].astype(F32)
    va = pa[d].astype(F32) + ra_c[x].astype(F32)
    for k in range(NX - 1):
        vg = vg + xg[k].astype(F32)
        va = va + xa[k].astype(F32)
    grad_out[0] = vg
    act_out[0] = va[:24]

    for c in zc[3]:
        c.wait_recv()
    left(lax.rem(t + 4, NZ))

    ch = []
    for k, off in enumerate(PEERS):
        hb[k + 1] = hf[k + 1].astype(BF)
        ch.append(send(hb.at[k + 1], rh.at[k], dp_dev(*neg(off))))
    load_b.wait()

    def brows(dx, dh):
        at = lax.rem(x + dx, NX) * CH + lax.rem(h + dh, 2) * HF
        return pl.ds(pl.multiple_of(at, HF), HF)

    acc[...] = nn(hf[0].astype(BF), bv[brows(0, 0), :])
    for k, off in enumerate(PEERS):
        ch[k].wait_recv()
        v = nn(rh[k], bv[brows(*off), :])
        if k < len(PEERS) - 1:
            acc[...] += v
        else:
            pre_out[0] = (acc[...] + v).astype(BF)
    for c in sends:
        c.wait_send()


N_COPIES = 7 + 6 * NP + 2 * 4 + 2 + 6 + NP + 7


def per_device(acts, outgrads, a_inverse, g_inverse):
    vmem = pl.BlockSpec(memory_space=pltpu.VMEM)
    anyw = pl.BlockSpec(memory_space=pl.ANY)
    V = pltpu.VMEM
    return pl.pallas_call(
        kernel,
        out_shape=(
            jax.ShapeDtypeStruct((1, 24, BLK), F32),
            jax.ShapeDtypeStruct((1, 48, BLK), F32),
            jax.ShapeDtypeStruct((1, HF, BLK), BF),
        ),
        in_specs=[anyw, anyw, vmem, anyw],
        out_specs=(vmem, vmem, vmem),
        scratch_shapes=[
            V((TOK, BLK), BF),
            V((TOK, BLK), BF),
            V((BLK, TOK), BF),
            V((BLK, BLK), BF),
            V((48, BLK // 2), BF),
            V((7, 48, BLK // 2), BF),
            V((NZ, HF, BLK), BF),
            V((2, HF, BLK), BF),
            V((2, HF, BLK), BF),
            V((2, HF, BLK), BF),
            V((2, HF, BLK), BF),
            V((2, HF, BLK), BF),
            V((2, HF, BLK), BF),
            V((2, HF, BLK), F32),
            V((2, HF, BLK), F32),
            V((HF, BLK), BF),
            V((HF, BLK), BF),
            V((HF, BLK), BF),
            V((8, 48, BLK), BF),
            V((8, 32, BLK), BF),
            V((NX, 48, BLK), BF),
            V((NX, 32, BLK), BF),
            V((NX - 1, 48, BLK), BF),
            V((NX - 1, 32, BLK), BF),
            V((NX - 1, 48, BLK), BF),
            V((NX - 1, 32, BLK), BF),
            V((8, HF, HF), F32),
            V((8, HF, HF), BF),
            V((7, HF, HF), BF),
            V((HF, BLK), F32),
            pltpu.SemaphoreType.DMA((6,)),
            pltpu.SemaphoreType.DMA((N_COPIES,)),
            pltpu.SemaphoreType.DMA((N_COPIES,)),
        ],
        compiler_params=pltpu.CompilerParams(
            collective_id=0, has_side_effects=True, vmem_limit_bytes=60 << 20
        ),
        cost_estimate=pl.CostEstimate(flops=9_500_000_000, bytes_accessed=13_000_000, transcendentals=0),
        name="precondition",
    )(acts, outgrads, a_inverse, g_inverse)


def solution(mesh):
    return jax.shard_map(
        per_device,
        mesh=mesh,
        in_specs=(
            P("dp", "owner"),
            P("dp", "tensor"),
            P("owner", ("dp", "tensor"), None),
            P("tensor", None, None),
        ),
        out_specs=(
            P("owner", ("dp", "tensor"), None),
            P("tensor", ("dp", "owner"), None),
            P("owner", "dp", "tensor"),
        ),
        check_vma=False,
    )
```

time: 1160 us -> 97.2 us (0.08)
  waiting for transfers between devices: 1090 us -> 0 us
  Pallas kernels: 0 us -> 91.1 us
  blocking collectives: 29.3 us -> 0 us
  matrix products: 27.4 us -> 0 us
  between operations: 13.8 us -> 0.64 us
    reduce_scatter x3 -> x0, waiting for transfers between devices: 1000 us -> none  [the longest x1 816 us: per_device(): lax.psum_scatter(cross(a_part, a_part) / total, ('dp', 'tensor'), scatter...]
    pallas_call x0 -> x1, Pallas kernels: none -> 91.1 us  [per_device(): pl.pallas_call(kernel, out_shape=(jax.ShapeDtypeStruct((1, 24, BLK), F32)...]
    all_gather x1 -> x0, waiting for transfers between devices: 87.3 us -> none  [per_device(): lax.all_gather(right, 'dp', axis=0, tiled=True)]
    all_gather x1 -> x0, blocking collectives: 29.3 us -> none  [per_device(): inverse_panel = lax.all_gather(a_inverse[0], 'tensor', axis=0, tiled=True)]
    dot_general x5 -> x0, matrix products: 27.4 us -> none  [the longest x3 18.6 us: cross(): lax.dot_general(left, right, (((0,), (0,)), ((), ())), preferred_element_...]
  transfers between devices with their start and end apart: 4 -> 0, of which waited for: 4 -> 0; matrix products, arithmetic and copies ran while one was open for 2% -> 0% of each run, Pallas kernels for 0% -> 0%
where the time goes in v1:
time: 97.2 us; the launch traced here: 96.9 us
  Pallas kernels  91.1 us (94%)
  local copies, waits for them, and re-layouts  5.19 us (5%)
    pallas_call x1, Pallas kernels, per_device(): pl.pallas_call(kernel, out_shape=(jax.ShapeDtypeStruct((1, 24, BLK), F32)...  91.1 us
    unnamed x3, local copies, waits for them, and re-layouts  5.19 us

profile of v1, /device:TPU:2, one launch (start us, length us, event | category | flops | bytes accessed | tf_op | source)
XLA Modules:
  0.0 96.9 jit_solution(5565509332196723012)
XLA Ops:
  0.6 91.1 %precondition.1 = (f32[1,24,1536]{2,1,0:T(8,128)}, f32[1,48,1536]{2,1,0:T(8,128)}, bf16[1,192,1536]{2,1,0:T(8,128)(2,1)}) custom-call(bf16[1024,1536]{1,0:T(8,128)(2,1)} %acts_h.1, bf16[1024,1536]{1,0:T(8,128)(2,1)} %og_h.1, bf16[1,24,1536]{2,1,0:T(8,128)(2,1)} %a_ref.1, bf16[1,1536,1536]{2,1,0:T(8,128)(2,1)} %b_h.1), custom_call_target="tpu_custom_call" | custom-call | flops 9500000256 | bytes 13000000 | tf_op jit(solution)/shard_map/precondition/pallas_call | solution.py:281
  91.7 1.6 %copy.10 = f32[1,24,1536]{2,1,0:T(8,128)} copy(f32[1,24,1536]{2,1,0:T(8,128)} %get-tuple-element.6) | data formatting | bytes 294912
  93.3 1.7 %copy.11 = f32[1,48,1536]{2,1,0:T(8,128)} copy(f32[1,48,1536]{2,1,0:T(8,128)} %get-tuple-element.7) | data formatting | bytes 589824
  95.0 1.9 %copy.12 = bf16[1,192,1536]{2,1,0:T(8,128)(2,1)} copy(bf16[1,192,1536]{2,1,0:T(8,128)(2,1)} %get-tuple-element.8) | data formatting | bytes 1179648

commit v2 on v1

--- a/solution.py
+++ b/solution.py
@@ -19,6 +19,7 @@
 PC = 512
 NP = BLK // PC
 PEERS = ((1, 0), (3, 0), (0, 1), (2, 0), (1, 1), (3, 1), (2, 1))
+PARTS = ((0, -1, 1, -2, 2, -3), (3, 4))
 
 
 def nt(a, b):
@@ -35,9 +36,10 @@
     acts, og, ogt, bv, a48, ra, abuf,
     u1, u2, u3, r1, r2, r3, keep, own, ys, yr, gt,
     pg, pa, rg, ra_c, sg, sa, xg, xa,
-    hf, hb, rh, acc,
+    hf, hb0, hb1, rh0, rh1, acc, total, asum,
     lsem, ssem, rsem,
 ):
+    hb, rh = (hb0, hb1), (rh0, rh1)
     d = lax.axis_index("dp")
     t = lax.axis_index("tensor")
     o = lax.axis_index("owner")
@@ -118,6 +120,25 @@
                 send(u1.at[1, :, pieces[p]], r1.at[1, :, pieces[p]], xm),
             ]
         )
+    up, down = z_dev(1), z_dev(-1)
+
+    def ring(slot, dev, part=None):
+        ref = abuf.at[slot] if part is None else abuf.at[slot, part]
+        return send(ref, ref, dev)
+
+    def unpack(k):
+        a_copies[k].wait_recv()
+        v = ra[k].astype(F32)
+        return jnp.concatenate([v[:24], v[24:]], axis=1)
+
+    zc = []
+    first = [a_ref[0].astype(F32)] + [unpack(k) for k in range(3)]
+    for n, w in enumerate((pl.ds(0, 96), pl.ds(96, 96))):
+        part = first if n == 0 else [unpack(k) for k in range(3, 7)]
+        abuf[t, w] = jnp.concatenate(part, axis=0).astype(BF)
+        zc.append([(ring(t, up, w), ring(t, down, w))])
+    zc = [zc[0] + zc[1]]
+
     c2 = [[None, None] for _ in range(NP)]
     for side in range(2):
         turn(1 + side)
@@ -130,24 +151,6 @@
             )
             keep[side, :, pieces[p]] = later
 
-    half = BLK // 2
-    rows = [a_ref[0].astype(F32)]
-    for k in range(len(PEERS)):
-        a_copies[k].wait_recv()
-        v = ra[k].astype(F32)
-        rows.append(jnp.concatenate([v[:24], v[24:]], axis=1))
-    abuf[t] = jnp.concatenate(rows, axis=0).astype(BF)
-    up, down = z_dev(1), z_dev(-1)
-
-    def ring(slot, dev, part=None):
-        ref = abuf.at[slot] if part is None else abuf.at[slot, part]
-        return send(ref, ref, dev)
-
-    def arrived(copy):
-        copy.wait_recv()
-
-    zc = [(ring(t, up), ring(t, down))]
-
     turn(3)
     gsel = jnp.concatenate(
         [ogt[pl.ds(pl.multiple_of(j * 192 + o * 48, 16), 48), :] for j in range(8)], axis=0
@@ -158,15 +161,15 @@
     yd = dp_dev(0, 1)
     there, here = (1 - h) * NX, h * NX
     cg = send(pg.at[pl.ds(there, NX)], rg, yd)
-    j = lax.broadcasted_iota(jnp.int32, (256, BLK), 0)
-    i = lax.broadcasted_iota(jnp.int32, (256, BLK), 1)
-    r = lax.rem(j, 32)
-    pick = (i == lax.div(j, 32) * 192 + t * 24 + r) & (r < 24)
+    j = lax.broadcasted_iota(jnp.int32, (192, BLK), 0)
+    i = lax.broadcasted_iota(jnp.int32, (192, BLK), 1)
+    pick = i == lax.div(j, 24) * 192 + t * 24 + lax.rem(j, 24)
     asel = nt(jnp.where(pick, 1.0, 0.0).astype(BF), acts[...]).astype(BF)
     for p in range(NP):
-        v = (nn(asel, acts[:, pieces[p]]) * SCALE).astype(BF)
-        pa[:, :, pieces[p]] = v.reshape(8, 32, PC)
-    ca = send(pa.at[pl.ds(there, NX)], ra_c, yd)
+        pa[:, pieces[p]] = (nn(asel, acts[:, pieces[p]]) * SCALE).astype(BF)
+    a_there = pl.ds(pl.multiple_of((1 - h) * 96, 96), 96)
+    a_here = pl.ds(pl.multiple_of(h * 96, 96), 96)
+    ca = send(pa.at[a_there], ra_c, yd)
     for p in range(NP):
         g = product(3, p)
         own[0, :, pieces[p]] = g[:HF]
@@ -186,26 +189,20 @@
         c3.append(row)
 
     def pass_on(s):
-        a, b = zc[s - 1]
+        prev = zc[s - 1]
         lower, upper = lax.rem(t - s + NZ, NZ), lax.rem(t + s, NZ)
-        a.wait_recv()
+        for a, _ in prev:
+            a.wait_recv()
         first, second = (None, None) if s < 3 else (pl.ds(0, 96), pl.ds(96, 96))
         fa = ring(lower, up, first)
-        b.wait_recv()
+        for _, b in prev:
+            b.wait_recv()
         fb = ring(upper, down, second)
-        zc.append((fa, fb))
+        zc.append([(fa, fb)])
 
     pass_on(1)
 
-    cg.wait_recv()
-    ca.wait_recv()
-    cx = []
-    for k in range(1, NX):
-        q = lax.rem(x + k, NX)
-        sg[k - 1] = (pg[here + q].astype(F32) + rg[q].astype(F32)).astype(BF)
-        sa[k - 1] = (pa[here + q].astype(F32) + ra_c[q].astype(F32)).astype(BF)
-        cx.append(send(sg.at[k - 1], xg.at[k - 1], dp_dev(k, 0)))
-        cx.append(send(sa.at[k - 1], xa.at[k - 1], dp_dev(k, 0)))
+    pass_on(2)
 
     cy = []
     for p in range(NP):
@@ -217,74 +214,116 @@
         ys[:, w] = (own[q, :, w] + r2[h, :, w].astype(F32) + r3[q, :, w].astype(F32)).astype(BF)
         cy.append(send(ys.at[:, w], yr.at[:, w], yd))
         own[h, :, w] = own[h, :, w] + r2[q, :, w].astype(F32) + r3[h, :, w].astype(F32)
-    pass_on(2)
+
+    cg.wait_recv()
+    ca.wait_recv()
+    cx = []
+    asum[...] = pa[a_here, :].astype(F32) + ra_c[...].astype(F32)
+    for k in range(1, NX):
+        q = lax.rem(x + k, NX)
+        sg[k - 1] = (pg[here + q].astype(F32) + rg[q].astype(F32)).astype(BF)
+        v = asum[pl.ds(pl.multiple_of(q * 24, 8), 24), :]
+        sa[k - 1] = jnp.concatenate([v[:, : BLK // 2], v[:, BLK // 2 :]], axis=0).astype(BF)
+        cx.append(send(sg.at[k - 1], xg.at[k - 1], dp_dev(k, 0)))
+        cx.append(send(sa.at[k - 1], xa.at[k - 1], dp_dev(k, 0)))
+
     for p in range(NP):
         w = pieces[p]
         cy[p].wait_recv()
         gt[:, w] = (own[h, :, w] + yr[:, w].astype(F32)).astype(BF)
 
-    def left(slot):
-        v = nt(abuf[slot], gt[...])
-        at = pl.ds(pl.multiple_of(slot * 24, 8), 24)
-        for k in range(8):
-            hf[k, at, :] = v[k * 24 : (k + 1) * 24]
-
-    for s in (0, -1, 1, -2, 2):
-        left(lax.rem(t + s + NZ, NZ))
+    def left(s):
+        hf[s % NZ] = nt(abuf[lax.rem(t + s + NZ, NZ)], gt[...])
+
+    def block(n, k):
+        part = PARTS[n]
+        v = jnp.concatenate([hf[s % NZ, k * 24 : (k + 1) * 24, :] for s in part], axis=0)
+        m = v.shape[0]
+        w = v[:, 128:]
+        w = jnp.concatenate([w[: m // 2], w[m // 2 :]], axis=1)
+        fill = jnp.zeros((hb[n].shape[1] - m - m // 2, 128), F32)
+        return jnp.concatenate([v[:, :128], w, fill], axis=0).astype(BF)
+
+    def exchange(n):
+        out = []
+        for k, off in enumerate(PEERS):
+            hb[n][k + 1] = block(n, k + 1)
+            out.append(send(hb[n].at[k + 1], rh[n].at[k], dp_dev(*neg(off))))
+        hb[n][0] = block(n, 0)
+        return out
+
+    def brows(dx, dh):
+        at = lax.rem(x + dx, NX) * CH + lax.rem(h + dh, 2) * HF
+        return pl.ds(pl.multiple_of(at, HF), HF)
+
+    def right(n, v, rows):
+        m = 24 * len(PARTS[n])
+        v = v.astype(F32)
+        w = v[m : m + m // 2]
+        w = jnp.concatenate([w[:, :64], w[:, 64:]], axis=0)
+        return nn(jnp.concatenate([v[:m], w], axis=1).astype(BF), bv[rows, :])
+
+    def finish(n, copies):
+        a = acc.at[pl.ds(0, 24 * len(PARTS[n]))]
+        a[...] = right(n, hb[n][0], brows(0, 0))
+        for k, off in enumerate(PEERS):
+            copies[k].wait_recv()
+            a[...] += right(n, rh[n][k], brows(*off))
+        for q, s in enumerate(PARTS[n]):
+            at = pl.ds(pl.multiple_of(lax.rem(t + s + NZ, NZ) * 24, 8), 24)
+            total[at, :] = acc[q * 24 : (q + 1) * 24]
+
+    for s in PARTS[0][:-1]:
+        left(s)
     pass_on(3)
-    for s in (-3, 3):
-        left(lax.rem(t + s + NZ, NZ))
+    left(PARTS[0][-1])
+    e0 = exchange(0)
+    left(PARTS[1][0])
+    for pair in zc[3]:
+        for c in pair:
+            c.wait_recv()
+    left(PARTS[1][1])
+    e1 = exchange(1)
+    load_b.wait()
+    finish(0, e0)
+    finish(1, e1)
+    pre_out[0] = total[...].astype(BF)
 
     for c in cx:
         c.wait_recv()
     vg = pg[d].astype(F32) + rg[x].astype(F32)
-    va = pa[d].astype(F32) + ra_c[x].astype(F32)
+    va = asum[pl.ds(pl.multiple_of(x * 24, 8), 24), :]
     for k in range(NX - 1):
         vg = vg + xg[k].astype(F32)
-        va = va + xa[k].astype(F32)
+        v = xa[k].astype(F32)
+        va = va + jnp.concatenate([v[:24], v[24:]], axis=1)
     grad_out[0] = vg
-    act_out[0] = va[:24]
-
-    for c in zc[3]:
-        c.wait_recv()
-    left(lax.rem(t + 4, NZ))
-
-    ch = []
-    for k, off in enumerate(PEERS):
-        hb[k + 1] = hf[k + 1].astype(BF)
-        ch.append(send(hb.at[k + 1], rh.at[k], dp_dev(*neg(off))))
-    load_b.wait()
-
-    def brows(dx, dh):
-        at = lax.rem(x + dx, NX) * CH + lax.rem(h + dh, 2) * HF
-        return pl.ds(pl.multiple_of(at, HF), HF)
-
-    acc[...] = nn(hf[0].astype(BF), bv[brows(0, 0), :])
-    for k, off in enumerate(PEERS):
-        ch[k].wait_recv()
-        v = nn(rh[k], bv[brows(*off), :])
-        if k < len(PEERS) - 1:
-            acc[...] += v
-        else:
-            pre_out[0] = (acc[...] + v).astype(BF)
+    act_out[0] = va
     for c in sends:
         c.wait_send()
 
 
-N_COPIES = 7 + 6 * NP + 2 * 4 + 2 + 6 + NP + 7
+N_COPIES = 7 + 6 * NP + 2 * 5 + 2 + 6 + NP + 14
+
+
+def store(a, b, c, a_out, b_out, c_out):
+    a_out[...] = a[...]
+    b_out[...] = b[...]
+    c_out[...] = c[...]
 
 
 def per_device(acts, outgrads, a_inverse, g_inverse):
     vmem = pl.BlockSpec(memory_space=pltpu.VMEM)
     anyw = pl.BlockSpec(memory_space=pl.ANY)
     V = pltpu.VMEM
-    return pl.pallas_call(
+    shapes = (
+        jax.ShapeDtypeStruct((1, 24, BLK), F32),
+        jax.ShapeDtypeStruct((1, 48, BLK), F32),
+        jax.ShapeDtypeStruct((1, HF, BLK), BF),
+    )
+    results = pl.pallas_call(
         kernel,
-        out_shape=(
-            jax.ShapeDtypeStruct((1, 24, BLK), F32),
-            jax.ShapeDtypeStruct((1, 48, BLK), F32),
-            jax.ShapeDtypeStruct((1, HF, BLK), BF),
-        ),
+        out_shape=shapes,
         in_specs=[anyw, anyw, vmem, anyw],
         out_specs=(vmem, vmem, vmem),
         scratch_shapes=[
@@ -307,17 +346,21 @@
             V((HF, BLK), BF),
             V((HF, BLK), BF),
             V((8, 48, BLK), BF),
-            V((8, 32, BLK), BF),
+            V((192, BLK), BF),
             V((NX, 48, BLK), BF),
-            V((NX, 32, BLK), BF),
+            V((96, BLK), BF),
             V((NX - 1, 48, BLK), BF),
-            V((NX - 1, 32, BLK), BF),
+            V((NX - 1, 48, BLK // 2), BF),
             V((NX - 1, 48, BLK), BF),
-            V((NX - 1, 32, BLK), BF),
+            V((NX - 1, 48, BLK // 2), BF),
             V((8, HF, HF), F32),
-            V((8, HF, HF), BF),
-            V((7, HF, HF), BF),
+            V((8, 224, 128), BF),
+            V((8, 80, 128), BF),
+            V((7, 224, 128), BF),
+            V((7, 80, 128), BF),
+            V((144, BLK), F32),
             V((HF, BLK), F32),
+            V((96, BLK), F32),
             pltpu.SemaphoreType.DMA((6,)),
             pltpu.SemaphoreType.DMA((N_COPIES,)),
             pltpu.SemaphoreType.DMA((N_COPIES,)),
@@ -328,6 +371,13 @@
         cost_estimate=pl.CostEstimate(flops=9_500_000_000, bytes_accessed=13_000_000, transcendentals=0),
         name="precondition",
     )(acts, outgrads, a_inverse, g_inverse)
+    return pl.pallas_call(
+        store,
+        out_shape=shapes,
+        in_specs=[vmem] * 3,
+        out_specs=(vmem,) * 3,
+        name="store",
+    )(*results)
 
 
 def solution(mesh):

time: 97.2 us -> 83.1 us (0.85)
  Pallas kernels: 91.1 us -> 82.3 us
  local copies, waits for them, and re-layouts: 5.19 us -> 0 us
    pallas_call x1 -> x2, Pallas kernels: 91.1 us -> 82.3 us  [the longest x1 80.1 us: per_device(): pl.pallas_call(kernel, out_shape=shapes, in_specs=[anyw, anyw, vmem, anyw...]
    unnamed x3 -> x0, local copies, waits for them, and re-layouts: 5.19 us -> none
where the time goes in v2:
time: 83.1 us; the launch traced here: 83 us
  Pallas kernels  82.3 us (99%)
    pallas_call x1, Pallas kernels, per_device(): pl.pallas_call(kernel, out_shape=shapes, in_specs=[anyw, anyw, vmem, anyw...  80.1 us
    pallas_call x1, Pallas kernels, per_device(): pl.pallas_call(store, out_shape=shapes, in_specs=[vmem] * 3, out_specs=(v...  2.21 us

profile of v2, /device:TPU:2, one launch (start us, length us, event | category | flops | bytes accessed | tf_op | source)
XLA Modules:
  0.0 83.0 jit_solution(10674423247606498744)
XLA Ops:
  0.6 80.1 %precondition.1 = (f32[1,24,1536]{2,1,0:T(8,128)}, f32[1,48,1536]{2,1,0:T(8,128)}, bf16[1,192,1536]{2,1,0:T(8,128)(2,1)}) custom-call(bf16[1024,1536]{1,0:T(8,128)(2,1)} %acts_h.1, bf16[1024,1536]{1,0:T(8,128)(2,1)} %og_h.1, bf16[1,24,1536]{2,1,0:T(8,128)(2,1)} %a_ref.1, bf16[1,1536,1536]{2,1,0:T(8,128)(2,1)} %b_h.1), custom_call_target="tpu_custom_call" | custom-call | flops 9500000256 | bytes 13000000 | tf_op jit(solution)/shard_map/precondition/pallas_call | solution.py:324
  80.8 2.2 %store.1 = (f32[1,24,1536]{2,1,0:T(8,128)}, f32[1,48,1536]{2,1,0:T(8,128)}, bf16[1,192,1536]{2,1,0:T(8,128)(2,1)}) custom-call(f32[1,24,1536]{2,1,0:T(8,128)} %get-tuple-element.6.a, f32[1,48,1536]{2,1,0:T(8,128)} %get-tuple-element.7.b, bf16[1,192,1536]{2,1,0:T(8,128)(2,1)} %get-tuple-element.8.c), custom_call_target="tpu_custom_call" | custom-call | tf_op jit(solution)/shard_map/store/pallas_call | solution.py:374

commit v3 on v2

--- a/solution.py
+++ b/solution.py
@@ -36,7 +36,7 @@
     acts, og, ogt, bv, a48, ra, abuf,
     u1, u2, u3, r1, r2, r3, keep, own, ys, yr, gt,
     pg, pa, rg, ra_c, sg, sa, xg, xa,
-    hf, hb0, hb1, rh0, rh1, acc, total, asum,
+    hf, hb0, hb1, rh0, rh1, acc, total, asum, fk, fs, fr, q1, w1, q2, w2,
     lsem, ssem, rsem,
 ):
     hb, rh = (hb0, hb1), (rh0, rh1)
@@ -108,9 +108,37 @@
         return nn(ogt[cols[k], :], acts[:, pieces[p]]) * SCALE
 
     turn(0)
+    up, down = z_dev(1), z_dev(-1)
+
+    def ring(slot, dev, part=None):
+        ref = abuf.at[slot] if part is None else abuf.at[slot, part]
+        return send(ref, ref, dev)
+
+    def unpack(k):
+        a_copies[k].wait_recv()
+        v = ra[k].astype(F32)
+        return jnp.concatenate([v[:24], v[24:]], axis=1)
+
+    def start_ring(n, part):
+        w = pl.ds(n * 96, 96)
+        abuf[t, w] = jnp.concatenate(part, axis=0).astype(BF)
+        return ring(t, up, w), ring(t, down, w)
+
+    z1 = [start_ring(0, [a_ref[0].astype(F32)] + [unpack(k) for k in range(3)])]
     load_acts.wait()
+    yd = dp_dev(0, 1)
+    last = pieces[NP - 1]
+    cf = []
+
+    def pair(k):
+        g = product(k, NP - 1)
+        fk[k, 0] = g[:HF]
+        fk[k, 1] = g[HF:]
+        fs[k] = fk[k, 1 - h].astype(BF)
+        cf.append(send(fs.at[k], fr.at[k], yd))
+
     c1 = []
-    for p in range(NP):
+    for p in range(NP - 1):
         g = product(0, p).astype(BF)
         u1[0, :, pieces[p]] = g[:HF]
         u1[1, :, pieces[p]] = g[HF:]
@@ -120,29 +148,15 @@
                 send(u1.at[1, :, pieces[p]], r1.at[1, :, pieces[p]], xm),
             ]
         )
-    up, down = z_dev(1), z_dev(-1)
-
-    def ring(slot, dev, part=None):
-        ref = abuf.at[slot] if part is None else abuf.at[slot, part]
-        return send(ref, ref, dev)
-
-    def unpack(k):
-        a_copies[k].wait_recv()
-        v = ra[k].astype(F32)
-        return jnp.concatenate([v[:24], v[24:]], axis=1)
-
-    zc = []
-    first = [a_ref[0].astype(F32)] + [unpack(k) for k in range(3)]
-    for n, w in enumerate((pl.ds(0, 96), pl.ds(96, 96))):
-        part = first if n == 0 else [unpack(k) for k in range(3, 7)]
-        abuf[t, w] = jnp.concatenate(part, axis=0).astype(BF)
-        zc.append([(ring(t, up, w), ring(t, down, w))])
-    zc = [zc[0] + zc[1]]
-
-    c2 = [[None, None] for _ in range(NP)]
+    pair(0)
+
+    z1.append(start_ring(1, [unpack(k) for k in range(3, 7)]))
+    zc = [z1]
+
+    c2 = [[None, None] for _ in range(NP - 1)]
     for side in range(2):
         turn(1 + side)
-        for p in range(NP):
+        for p in range(NP - 1):
             g = product(1 + side, p)
             now, later = (g[HF:], g[:HF]) if side == 0 else (g[:HF], g[HF:])
             u2[side, :, pieces[p]] = now.astype(BF)
@@ -150,15 +164,16 @@
                 u2.at[side, :, pieces[p]], r2.at[side, :, pieces[p]], (xp, xm)[side]
             )
             keep[side, :, pieces[p]] = later
-
+        pair(1 + side)
     turn(3)
+    pair(3)
+
     gsel = jnp.concatenate(
         [ogt[pl.ds(pl.multiple_of(j * 192 + o * 48, 16), 48), :] for j in range(8)], axis=0
     )
     for p in range(NP):
         r = (nn(gsel, og[:, pieces[p]]) * SCALE).astype(BF)
         pg[:, :, pieces[p]] = r.reshape(8, 48, PC)
-    yd = dp_dev(0, 1)
     there, here = (1 - h) * NX, h * NX
     cg = send(pg.at[pl.ds(there, NX)], rg, yd)
     j = lax.broadcasted_iota(jnp.int32, (192, BLK), 0)
@@ -170,13 +185,13 @@
     a_there = pl.ds(pl.multiple_of((1 - h) * 96, 96), 96)
     a_here = pl.ds(pl.multiple_of(h * 96, 96), 96)
     ca = send(pa.at[a_there], ra_c, yd)
-    for p in range(NP):
+    for p in range(NP - 1):
         g = product(3, p)
         own[0, :, pieces[p]] = g[:HF]
         own[1, :, pieces[p]] = g[HF:]
 
     c3 = []
-    for p in range(NP):
+    for p in range(NP - 1):
         row = []
         for side in range(2):
             c1[p][side].wait_recv()
@@ -202,10 +217,31 @@
 
     pass_on(1)
 
+    for c in cf:
+        c.wait_recv()
+
+    def pair_sum(k):
+        return fk[k, h] + fr[k].astype(F32)
+
+    v = pair_sum(0).astype(BF)
+    q1[0] = v[: HF // 2]
+    q1[1] = v[HF // 2 :]
+    d1 = [send(q1.at[i], w1.at[i], (xp, xm)[i]) for i in range(2)]
     pass_on(2)
+    d2 = []
+    for i in range(2):
+        d1[i].wait_recv()
+        v = pair_sum(1 + i)
+        top, bottom = v[: HF // 2], v[HF // 2 :]
+        if i == 0:
+            top = top + w1[0].astype(F32)
+        else:
+            bottom = bottom + w1[1].astype(F32)
+        q2[i] = jnp.concatenate([top, bottom], axis=0).astype(BF)
+        d2.append(send(q2.at[i], w2.at[i], (xp, xm)[i]))
 
     cy = []
-    for p in range(NP):
+    for p in range(NP - 1):
         for side in range(2):
             c2[p][side].wait_recv()
             c3[p][side].wait_recv()
@@ -227,10 +263,15 @@
         cx.append(send(sg.at[k - 1], xg.at[k - 1], dp_dev(k, 0)))
         cx.append(send(sa.at[k - 1], xa.at[k - 1], dp_dev(k, 0)))
 
-    for p in range(NP):
+    pass_on(3)
+    for p in range(NP - 1):
         w = pieces[p]
         cy[p].wait_recv()
         gt[:, w] = (own[h, :, w] + yr[:, w].astype(F32)).astype(BF)
+
+    for c in d2:
+        c.wait_recv()
+    gt[:, last] = (pair_sum(3) + w2[0].astype(F32) + w2[1].astype(F32)).astype(BF)
 
     def left(s):
         hf[s % NZ] = nt(abuf[lax.rem(t + s + NZ, NZ)], gt[...])
@@ -275,7 +316,6 @@
 
     for s in PARTS[0][:-1]:
         left(s)
-    pass_on(3)
     left(PARTS[0][-1])
     e0 = exchange(0)
     left(PARTS[1][0])
@@ -286,9 +326,6 @@
     e1 = exchange(1)
     load_b.wait()
     finish(0, e0)
-    finish(1, e1)
-    pre_out[0] = total[...].astype(BF)
-
     for c in cx:
         c.wait_recv()
     vg = pg[d].astype(F32) + rg[x].astype(F32)
@@ -299,11 +336,13 @@
         va = va + jnp.concatenate([v[:24], v[24:]], axis=1)
     grad_out[0] = vg
     act_out[0] = va
+    finish(1, e1)
+    pre_out[0] = total[...].astype(BF)
     for c in sends:
         c.wait_send()
 
 
-N_COPIES = 7 + 6 * NP + 2 * 5 + 2 + 6 + NP + 14
+N_COPIES = 7 + 7 * (NP - 1) + 8 + 2 * 5 + 2 + 6 + 14
 
 
 def store(a, b, c, a_out, b_out, c_out):
@@ -361,6 +400,13 @@
             V((144, BLK), F32),
             V((HF, BLK), F32),
             V((96, BLK), F32),
+            V((NX, 2, HF, PC), F32),
+            V((NX, HF, PC), BF),
+            V((NX, HF, PC), BF),
+            V((2, HF // 2, PC), BF),
+            V((2, HF // 2, PC), BF),
+            V((2, HF, PC), BF),
+            V((2, HF, PC), BF),
             pltpu.SemaphoreType.DMA((6,)),
             pltpu.SemaphoreType.DMA((N_COPIES,)),
             pltpu.SemaphoreType.DMA((N_COPIES,)),

time: 83.1 us -> 79.3 us (0.954); the launches traced: 83 us -> 78 us
  Pallas kernels: 82.3 us -> 77.4 us
    pallas_call x1, Pallas kernels: 80.1 us -> 75.2 us  [per_device(): pl.pallas_call(kernel, out_shape=shapes, in_specs=[anyw, anyw, vmem, anyw...]
where the time goes in v3:
time: 79.3 us; the launch traced here: 78 us
  Pallas kernels  77.4 us (98%)
    pallas_call x1, Pallas kernels, per_device(): pl.pallas_call(kernel, out_shape=shapes, in_specs=[anyw, anyw, vmem, anyw...  75.2 us
    pallas_call x1, Pallas kernels, per_device(): pl.pallas_call(store, out_shape=shapes, in_specs=[vmem] * 3, out_specs=(v...  2.21 us

profile of v3, /device:TPU:2, one launch (start us, length us, event | category | flops | bytes accessed | tf_op | source)
XLA Modules:
  0.0 78.0 jit_solution(3148972488237941717)
XLA Ops:
  0.6 75.2 %precondition.1 = (f32[1,24,1536]{2,1,0:T(8,128)}, f32[1,48,1536]{2,1,0:T(8,128)}, bf16[1,192,1536]{2,1,0:T(8,128)(2,1)}) custom-call(bf16[1024,1536]{1,0:T(8,128)(2,1)} %acts_h.1, bf16[1024,1536]{1,0:T(8,128)(2,1)} %og_h.1, bf16[1,24,1536]{2,1,0:T(8,128)(2,1)} %a_ref.1, bf16[1,1536,1536]{2,1,0:T(8,128)(2,1)} %b_h.1), custom_call_target="tpu_custom_call" | custom-call | flops 9500000256 | bytes 13000000 | tf_op jit(solution)/shard_map/precondition/pallas_call | solution.py:363
  75.8 2.2 %store.1 = (f32[1,24,1536]{2,1,0:T(8,128)}, f32[1,48,1536]{2,1,0:T(8,128)}, bf16[1,192,1536]{2,1,0:T(8,128)(2,1)}) custom-call(f32[1,24,1536]{2,1,0:T(8,128)} %get-tuple-element.6.a, f32[1,48,1536]{2,1,0:T(8,128)} %get-tuple-element.7.b, bf16[1,192,1536]{2,1,0:T(8,128)(2,1)} %get-tuple-element.8.c), custom_call_target="tpu_custom_call" | custom-call | tf_op jit(solution)/shard_map/store/pallas_call | solution.py:420

commit v4 on v3

--- a/solution.py
+++ b/solution.py
@@ -167,6 +167,38 @@
         pair(1 + side)
     turn(3)
     pair(3)
+
+    for p in range(NP - 1):
+        g = product(3, p)
+        own[0, :, pieces[p]] = g[:HF]
+        own[1, :, pieces[p]] = g[HF:]
+
+    c3 = []
+    for p in range(NP - 1):
+        row = []
+        for side in range(2):
+            c1[p][side].wait_recv()
+            u3[side, :, pieces[p]] = (
+                keep[side, :, pieces[p]] + r1[side, :, pieces[p]].astype(F32)
+            ).astype(BF)
+            row.append(
+                send(u3.at[side, :, pieces[p]], r3.at[side, :, pieces[p]], (xp, xm)[side])
+            )
+        c3.append(row)
+
+    def pass_on(s):
+        prev = zc[s - 1]
+        lower, upper = lax.rem(t - s + NZ, NZ), lax.rem(t + s, NZ)
+        for a, _ in prev:
+            a.wait_recv()
+        first, second = (None, None) if s < 3 else (pl.ds(0, 96), pl.ds(96, 96))
+        fa = ring(lower, up, first)
+        for _, b in prev:
+            b.wait_recv()
+        fb = ring(upper, down, second)
+        zc.append([(fa, fb)])
+
+    pass_on(1)
 
     gsel = jnp.concatenate(
         [ogt[pl.ds(pl.multiple_of(j * 192 + o * 48, 16), 48), :] for j in range(8)], axis=0
@@ -185,38 +217,6 @@
     a_there = pl.ds(pl.multiple_of((1 - h) * 96, 96), 96)
     a_here = pl.ds(pl.multiple_of(h * 96, 96), 96)
     ca = send(pa.at[a_there], ra_c, yd)
-    for p in range(NP - 1):
-        g = product(3, p)
-        own[0, :, pieces[p]] = g[:HF]
-        own[1, :, pieces[p]] = g[HF:]
-
-    c3 = []
-    for p in range(NP - 1):
-        row = []
-        for side in range(2):
-            c1[p][side].wait_recv()
-            u3[side, :, pieces[p]] = (
-                keep[side, :, pieces[p]] + r1[side, :, pieces[p]].astype(F32)
-            ).astype(BF)
-            row.append(
-                send(u3.at[side, :, pieces[p]], r3.at[side, :, pieces[p]], (xp, xm)[side])
-            )
-        c3.append(row)
-
-    def pass_on(s):
-        prev = zc[s - 1]
-        lower, upper = lax.rem(t - s + NZ, NZ), lax.rem(t + s, NZ)
-        for a, _ in prev:
-            a.wait_recv()
-        first, second = (None, None) if s < 3 else (pl.ds(0, 96), pl.ds(96, 96))
-        fa = ring(lower, up, first)
-        for _, b in prev:
-            b.wait_recv()
-        fb = ring(upper, down, second)
-        zc.append([(fa, fb)])
-
-    pass_on(1)
-
     for c in cf:
         c.wait_recv()
 

time: 79.3 us -> 79.3 us (level)
  no operation moved by 1% of the time
where the time goes in v4:
time: 79.3 us; the launch traced here: 78 us
  Pallas kernels  77.4 us (98%)
    pallas_call x1, Pallas kernels, per_device(): pl.pallas_call(kernel, out_shape=shapes, in_specs=[anyw, anyw, vmem, anyw...  75.2 us
    pallas_call x1, Pallas kernels, per_device(): pl.pallas_call(store, out_shape=shapes, in_specs=[vmem] * 3, out_specs=(v...  2.21 us

profile of v4, /device:TPU:2, one launch (start us, length us, event | category | flops | bytes accessed | tf_op | source)
XLA Modules:
  0.0 78.0 jit_solution(13958411021474451529)
XLA Ops:
  0.6 75.2 %precondition.1 = (f32[1,24,1536]{2,1,0:T(8,128)}, f32[1,48,1536]{2,1,0:T(8,128)}, bf16[1,192,1536]{2,1,0:T(8,128)(2,1)}) custom-call(bf16[1024,1536]{1,0:T(8,128)(2,1)} %acts_h.1, bf16[1024,1536]{1,0:T(8,128)(2,1)} %og_h.1, bf16[1,24,1536]{2,1,0:T(8,128)(2,1)} %a_ref.1, bf16[1,1536,1536]{2,1,0:T(8,128)(2,1)} %b_h.1), custom_call_target="tpu_custom_call" | custom-call | flops 9500000256 | bytes 13000000 | tf_op jit(solution)/shard_map/precondition/pallas_call | solution.py:363
  75.8 2.2 %store.1 = (f32[1,24,1536]{2,1,0:T(8,128)}, f32[1,48,1536]{2,1,0:T(8,128)}, bf16[1,192,1536]{2,1,0:T(8,128)(2,1)}) custom-call(f32[1,24,1536]{2,1,0:T(8,128)} %get-tuple-element.6.a, f32[1,48,1536]{2,1,0:T(8,128)} %get-tuple-element.7.b, bf16[1,192,1536]{2,1,0:T(8,128)(2,1)} %get-tuple-element.8.c), custom_call_target="tpu_custom_call" | custom-call | tf_op jit(solution)/shard_map/store/pallas_call | solution.py:420
